TPU v7x, 512 devices: a whole 4x8x8 slice. The times are simulated.
512 devices in a mesh: grp: 8 (over z_hi, core), seq: 64 (over y, z_lo, x).
Axes of the slice: x: 4, y: 8, z: 8 (z_hi: 4, z_lo: 2; z = z_hi * 2 + z_lo), core: 2. Of those that a mesh axis runs over, the one named last changes fastest.
Arguments:
- queries: bfloat16 [65536, 3072], P(('grp', 'seq'))
- keys: bfloat16 [65536, 3072], P(('grp', 'seq'))
- values: bfloat16 [65536, 3072], P(('grp', 'seq')), may hold values from -6 to 6
- head_order: int32 [24], replicated, may hold values from 0 to 23, each once
- key_blocks: int32 [128, 6], replicated, may hold values from 0 to 127, as said below
- block_count: int32 [128], replicated, may hold values from 2 to 6, as said below
Outputs:
- attended: bfloat16 [65536, 3072], P(('grp', 'seq'))
Inputs may be any that keep to these rules, and one draw needn't show every extreme that they name: `key_blocks`: each row lists distinct frames; entry 0 is the row's own frame; every entry lies within 3 frames of the row's frame on the closed loop of 128 frames. `block_count`: some frame uses all 6 entries.
All inputs are finite; a program needn't handle non-finite values.
Results may differ from a plain program's by a relative error of at most 0.009.
Values may be sent and summed in bfloat16 or wider, within the bound.
No kernel may reach another device: no remote copies, remote signals or barrier semaphores. Data moves between devices by JAX's collectives and lax.ppermute only.
A program may use at most 64 MiB of HBM per device.

v0:
```python
import jax
import jax.numpy as jnp
from jax import lax
from jax.sharding import PartitionSpec as P

HT = 8
W = 3
NB = 6
FS = 4


def partner(block, axis, distance):
    count = lax.axis_size(axis)
    route = []
    for low in range(count):
        high = low | 1 << distance
        if high != low and high < count:
            route += [(low, high), (high, low)]
    return lax.ppermute(block, axis, route)


def from_behind(array, axis, by):
    count = lax.axis_size(axis)
    return lax.ppermute(array, axis, [(i, (i + by) % count) for i in range(count)])


def soft_weights(scores):
    top = jnp.max(scores, axis=-1, keepdims=True)
    expo = jnp.exp(scores - top)
    return (expo / jnp.sum(expo, axis=-1, keepdims=True)).astype(jnp.bfloat16)


def temporal_attend(tq, tk, tv, scale):
    scores = jnp.einsum("fphd,gphd->phfg", tq, tk, preferred_element_type=jnp.float32) * scale
    weights = soft_weights(scores)
    out = jnp.einsum("phfg,gphd->fphd", weights, tv, preferred_element_type=jnp.float32)
    return out.astype(jnp.bfloat16)


def frame_exchange(source, where, sender):
    bit_total = FS.bit_length() - 1
    shape = source.shape
    current = source.reshape(shape[:where] + (2,) * bit_total + shape[where + 1 :])
    position = lax.axis_index("seq")
    for bit in range(bit_total):
        axis_at = where + (bit_total - 1 - bit)
        mine_bit = position >> bit & 1
        mine = lax.dynamic_index_in_dim(current, mine_bit, axis_at, keepdims=True)
        other = lax.dynamic_index_in_dim(current, 1 - mine_bit, axis_at, keepdims=True)
        arrived = sender(other, bit)
        current = jnp.where(
            mine_bit == 0,
            jnp.concatenate([mine, arrived], axis_at),
            jnp.concatenate([arrived, mine], axis_at),
        )
    return current.reshape(shape)


def local(queries, keys, values, head_order, key_blocks, block_count):
    rows = queries.shape[0]
    width = head_order.shape[0]
    depth = queries.shape[1] // width
    spatial_count = width - HT
    group_heads = spatial_count // FS
    scale = depth ** (-0.5)
    seq_total = lax.axis_size("seq")
    grp_total = lax.axis_size("grp")
    frames = grp_total * seq_total // FS
    frame = (lax.axis_index("grp") * seq_total + lax.axis_index("seq")) // FS
    q_three = queries.reshape(rows, width, depth)
    k_three = keys.reshape(rows, width, depth)
    v_three = values.reshape(rows, width, depth)
    temporal_ids = head_order[:HT]
    spatial_ids = head_order[HT:]
    tq = jnp.take(q_three, temporal_ids, axis=1)[None]
    tk = jnp.take(k_three, temporal_ids, axis=1)[None]
    tv = jnp.take(v_three, temporal_ids, axis=1)[None]
    piece_rows = rows // seq_total
    head_share = HT // grp_total
    gq, gk, gv = (
        lax.all_to_all(
            lax.all_to_all(tq, "seq", split_axis=1, concat_axis=0, tiled=True),
            "grp",
            split_axis=2,
            concat_axis=0,
            tiled=True,
        ),
        lax.all_to_all(
            lax.all_to_all(tk, "seq", split_axis=1, concat_axis=0, tiled=True),
            "grp",
            split_axis=2,
            concat_axis=0,
            tiled=True,
        ),
        lax.all_to_all(
            lax.all_to_all(tv, "seq", split_axis=1, concat_axis=0, tiled=True),
            "grp",
            split_axis=2,
            concat_axis=0,
            tiled=True,
        ),
    )
    shaped = [a.reshape(frames, FS * piece_rows, head_share, depth) for a in (gq, gk, gv)]
    result = temporal_attend(shaped[0], shaped[1], shaped[2], scale)
    result = result.reshape(grp_total * seq_total, piece_rows, head_share, depth)
    temporal_part = lax.all_to_all(
        lax.all_to_all(result, "grp", split_axis=0, concat_axis=2, tiled=True),
        "seq",
        split_axis=0,
        concat_axis=1,
        tiled=True,
    )[0]
    columns = group_heads * depth
    s_query = jnp.take(q_three, spatial_ids, axis=1).reshape(rows, FS, columns)
    s_key = jnp.take(k_three, spatial_ids, axis=1).reshape(rows, FS, columns)
    s_value = jnp.take(v_three, spatial_ids, axis=1).reshape(rows, FS, columns)
    outgoing = jnp.stack([s_query, s_key, s_value])
    incoming = frame_exchange(outgoing, 2, lambda part, bit: partner(part, "seq", bit))
    positions = rows * FS
    query_rows = incoming[0].reshape(positions, columns)
    paired = incoming[1:3].reshape(2, positions, columns)
    nearby = {0: paired}
    for distance in range(-W, W + 1):
        if distance != 0:
            nearby[distance] = from_behind(paired, ("grp", "seq"), -distance * FS)
    stacked = jnp.stack([nearby[distance] for distance in range(-W, W + 1)])
    listed = lax.dynamic_index_in_dim(key_blocks, frame, 0, keepdims=False)
    count = lax.dynamic_index_in_dim(block_count, frame, 0, keepdims=False)
    offset = (listed - frame) % frames
    offset = jnp.where(offset > W, offset - frames, offset)
    slot_index = offset + W
    live = jnp.arange(NB) < count
    member = jnp.any(
        (slot_index[:, None] == jnp.arange(2 * W + 1)[None, :]) & live[:, None], axis=0
    )
    slot_total = stacked.shape[0]
    key_rows = stacked[:, 0].reshape(slot_total * positions, columns)
    value_rows = stacked[:, 1].reshape(slot_total * positions, columns)
    keep_rows = jnp.repeat(member, positions)

    def one_head(head):
        start = head * depth
        q_head = lax.dynamic_slice_in_dim(query_rows, start, depth, 1)
        k_head = lax.dynamic_slice_in_dim(key_rows, start, depth, 1)
        v_head = lax.dynamic_slice_in_dim(value_rows, start, depth, 1)
        scores = jnp.einsum("pd,kd->pk", q_head, k_head, preferred_element_type=jnp.float32) * scale
        scores = jnp.where(keep_rows[None, :], scores, -jnp.inf)
        weights = soft_weights(scores)
        return jnp.dot(weights, v_head, preferred_element_type=jnp.float32).astype(jnp.bfloat16)

    head_outs = (
        lax.map(one_head, jnp.arange(group_heads)).transpose(1, 0, 2).reshape(rows, FS, columns)
    )
    returned = frame_exchange(head_outs, 1, lambda part, bit: partner(part, "seq", bit))
    spatial_part = returned.reshape(rows, spatial_count, depth)
    joined = jnp.concatenate([temporal_part, spatial_part], axis=1)
    inverse = jnp.argsort(head_order)
    return jnp.take(joined, inverse, axis=1).reshape(rows, width * depth)


def solution(mesh):
    return jax.shard_map(
        local,
        mesh=mesh,
        in_specs=(
            P(("grp", "seq"), None),
            P(("grp", "seq"), None),
            P(("grp", "seq"), None),
            P(),
            P(),
            P(),
        ),
        out_specs=P(("grp", "seq"), None),
        check_vma=False,
    )
```

profile of v0, /device:TPU:1, one launch (start us, length us, event | category | flops | bytes accessed | tf_op | source)
XLA Modules:
  0.0 375.1 jit_solution(12233559940479724392)
XLA Ops:
  8.9 1.9 select_bitcast_fusion.4
  11.7 13.2 %all-to-all-start.2 = ((bf16[1,128,8,128]{3,2,0,1:T(8,128)(2,1)}), bf16[1,128,8,128]{3,2,0,1:T(8,128)(2,1)}, u32[]{:S(2)}, u32[]{:S(2)}) async-start(bf16[1,128,8,128]{3,2,0,1:T(8,128)(2,1)} %copy.151), calls=%async_computation.2 | async-start | bytes 524288 | tf_op jit(solution)/shard_map/all_to_all | solution.py:82
  30.1 2.8 collective-permute-start
  35.9 9.4 %all-to-all-start.4 = ((bf16[1,128,8,128]{3,2,0,1:T(8,128)(2,1)}), bf16[1,128,8,128]{3,2,0,1:T(8,128)(2,1)S(1)}, u32[]{:S(2)}, u32[]{:S(2)}) async-start(bf16[1,128,8,128]{3,2,0,1:T(8,128)(2,1)} %copy.155), calls=%async_computation.4 | async-start | bytes 524288 | tf_op jit(solution)/shard_map/all_to_all | solution.py:89
  46.2 9.7 %all-to-all-done.4 = bf16[1,128,8,128]{3,2,0,1:T(8,128)(2,1)S(1)} async-done(((bf16[1,128,8,128]{3,2,0,1:T(8,128)(2,1)}), bf16[1,128,8,128]{3,2,0,1:T(8,128)(2,1)S(1)}, u32[]{:S(2)}, u32[]{:S(2)}) %all-to-all-start.4) | async-done | bytes 262176 | tf_op jit(solution)/shard_map/all_to_all | solution.py:89
  55.9 7.2 %all-to-all-start = ((bf16[1,128,8,128]{3,2,0,1:T(8,128)(2,1)}), bf16[1,128,8,128]{3,2,0,1:T(8,128)(2,1)S(1)}, u32[]{:S(2)}, u32[]{:S(2)}) async-start(bf16[1,128,8,128]{3,2,0,1:T(8,128)(2,1)} %copy.147), calls=%async_computation | async-start | bytes 524288 | tf_op jit(solution)/shard_map/all_to_all | solution.py:96
  64.9 4.4 %collective-permute-start.1 = (bf16[3,128,1,2,512]{1,4,3,2,0:T(8,128)(2,1)S(1)}, bf16[3,128,1,2,512]{1,4,3,2,0:T(8,128)(2,1)S(1)}, u32[]{:S(2)}, u32[]{:S(2)}) collective-permute-start(bf16[3,128,1,2,512]{1,4,3,2,0:T(8,128)(2,1)S(1)} %get-tuple-element.87), channel_id=1, source_target_pairs={{0,2},{2,0},{1,3},{3,1},{4,6},{6,4},{5,7},{7,5},{8,10},{10,8},{9,1... | collective-permute-start | bytes 2359304 | tf_op jit(solution)/shard_map/ppermute | solution.py:19
  69.3 1.9 copy.152
  71.2 3.1 all-to-all-done
  74.2 12.9 %all-to-all-start.3 = ((bf16[64,2,8,128]{3,1,0,2:T(2,128)(2,1)}), bf16[64,2,8,128]{3,1,0,2:T(2,128)(2,1)S(1)}, u32[]{:S(2)}, u32[]{:S(2)}) async-start(bf16[64,2,8,128]{3,1,0,2:T(2,128)(2,1)} %copy.152), calls=%async_computation.3 | async-start | bytes 524288 | tf_op jit(solution)/shard_map/all_to_all | solution.py:81
  88.1 9.2 %all-to-all-done.3 = bf16[64,2,8,128]{3,1,0,2:T(2,128)(2,1)S(1)} async-done(((bf16[64,2,8,128]{3,1,0,2:T(2,128)(2,1)}), bf16[64,2,8,128]{3,1,0,2:T(2,128)(2,1)S(1)}, u32[]{:S(2)}, u32[]{:S(2)}) %all-to-all-start.3) | async-done | bytes 262176 | tf_op jit(solution)/shard_map/all_to_all | solution.py:81
  97.3 5.6 %all-to-all-start.5 = ((bf16[64,2,8,128]{3,1,0,2:T(2,128)(2,1)}), bf16[64,2,8,128]{3,1,0,2:T(2,128)(2,1)S(1)}, u32[]{:S(2)}, u32[]{:S(2)}) async-start(bf16[64,2,8,128]{3,1,0,2:T(2,128)(2,1)} %copy.156), calls=%async_computation.5 | async-start | bytes 524288 | tf_op jit(solution)/shard_map/all_to_all | solution.py:88
  106.5 2.6 copy.173
  109.1 2.3 collective-permute-start.2
  112.3 2.6 collective-permute-start.3
  116.4 7.8 %all-to-all-start.1 = ((bf16[64,2,8,128]{3,1,0,2:T(2,128)(2,1)}), bf16[64,2,8,128]{3,1,0,2:T(2,128)(2,1)S(1)}, u32[]{:S(2)}, u32[]{:S(2)}) async-start(bf16[64,2,8,128]{3,1,0,2:T(2,128)(2,1)} %copy.148), calls=%async_computation.1 | async-start | bytes 524288 | tf_op jit(solution)/shard_map/all_to_all | solution.py:95
  124.3 2.8 collective-permute-start.4
  128.6 4.9 %collective-permute-start.5 = (bf16[2,512,512]{2,0,1:T(2,128)(2,1)S(1)}, bf16[2,512,512]{2,0,1:T(2,128)(2,1)}, u32[]{:S(2)}, u32[]{:S(2)}) collective-permute-start(bf16[2,512,512]{2,0,1:T(2,128)(2,1)S(1)} %bitcast.93), channel_id=1, source_target_pairs={{0,508},{1,509},{2,510},{3,511},{4,0},{5,1},{6,2},{7,3},{8,4},{9,5... | collective-permute-start | bytes 3145736 | tf_op jit(solution)/shard_map/ppermute | solution.py:24
  133.5 94.2 %all-to-all-done.1 = bf16[64,2,8,128]{3,1,0,2:T(2,128)(2,1)S(1)} async-done(((bf16[64,2,8,128]{3,1,0,2:T(2,128)(2,1)}), bf16[64,2,8,128]{3,1,0,2:T(2,128)(2,1)S(1)}, u32[]{:S(2)}, u32[]{:S(2)}) %all-to-all-start.1) | async-done | bytes 262176 | tf_op jit(solution)/shard_map/all_to_all | solution.py:95
  230.1 3.9 %all-to-all-start.6 = ((bf16[512,2,1,128]{3,1,2,0:T(2,128)(2,1)}), bf16[512,2,1,128]{3,1,2,0:T(2,128)(2,1)S(1)}, u32[]{:S(2)}, u32[]{:S(2)}) async-start(bf16[512,2,1,128]{3,1,2,0:T(2,128)(2,1)} %bitcast.25), calls=%async_computation.6 | async-start | bytes 524288 | tf_op jit(solution)/shard_map/all_to_all | solution.py:107
  234.0 1.9 collective-permute-start.7
  236.7 2.1 collective-permute-start.6
  238.8 1.9 bitcast_dynamic-update-slice_fusion.5
  240.7 2.0 bitcast_dynamic-update-slice_fusion.4
  242.7 2.8 collective-permute-done.4
  245.5 2.0 bitcast_dynamic-update-slice_fusion.3
  248.3 2.0 bitcast_dynamic-update-slice_fusion.2
  250.3 36.0 %collective-permute-done.6 = bf16[2,512,512]{2,0,1:T(2,128)(2,1)S(1)} collective-permute-done((bf16[2,512,512]{2,0,1:T(2,128)(2,1)S(1)}, bf16[2,512,512]{2,0,1:T(2,128)(2,1)S(1)}, u32[]{:S(2)}, u32[]{:S(2)}) %collective-permute-start.6) | collective-permute-done | bytes 1048608 | tf_op jit(solution)/shard_map/ppermute | solution.py:24
  287.1 2.0 bitcast_dynamic-update-slice_fusion
  289.2 11.4 %fusion.31 = (bf16[7,1,512,512]{3,1,2,0:T(2,128)(2,1)}, bf16[7,1,512,512]{3,1,2,0:T(2,128)(2,1)S(1)}) fusion(bf16[7,2,512,512]{3,1,2,0:T(2,128)(2,1)S(1)} %bitcast_dynamic-update-slice_fusion), kind=kLoop, calls=%fused_computation.84 | loop fusion | bytes 14680064 | tf_op jit(solution)/shard_map/slice | solution.py:138
  300.6 6.1 %copy.182 = bf16[7,1,512,512]{3,2,1,0:T(8,128)(2,1)} copy(bf16[7,1,512,512]{3,1,2,0:T(2,128)(2,1)} %get-tuple-element.84) | data formatting | bytes 7340032
  306.7 2.9 copy.181
  309.6 30.3 %while.11 = (s32[]{:T(128)}, bf16[4,512,128]{2,1,0:T(8,128)(2,1)S(1)}, s32[4]{0:T(128)S(1)}, bf16[512,512]{1,0:T(8,128)(2,1)S(1)}, bf16[3584,512]{1,0:T(8,128)(2...) while((s32[]{:T(128)}, ...), condition=%wide.region_7.10_spmd.clone, body=%wide.region_4.9_spmd.clone.sunk | while | flops 954268672 | bytes 24143548 | solution.py:152
  310.9 2.5 fusion.43
  314.5 2.6 fusion.45
  318.5 2.5 fusion.43
  322.1 2.6 fusion.45
  326.1 2.5 fusion.43
  329.7 2.6 fusion.45
  333.6 2.5 fusion.43
  337.3 2.6 fusion.45
  341.6 1.9 collective-permute-start.8
  344.5 9.4 %all-to-all-start.7 = ((bf16[64,2,8,128]{3,2,1,0:T(8,128)(2,1)}), bf16[64,2,8,128]{3,2,1,0:T(8,128)(2,1)S(1)}, u32[]{:S(2)}, u32[]{:S(2)}) async-start(bf16[64,2,8,128]{3,2,1,0:T(8,128)(2,1)} %copy.164), calls=%async_computation.7 | async-start | bytes 524288 | tf_op jit(solution)/shard_map/all_to_all | solution.py:106
  353.8 3.0 collective-permute-done.8
  356.8 2.3 broadcast_select_fusion
  359.5 2.6 collective-permute-start.9
  362.3 4.4 %all-to-all-done.7 = bf16[64,2,8,128]{3,2,1,0:T(8,128)(2,1)S(1)} async-done(((bf16[64,2,8,128]{3,2,1,0:T(8,128)(2,1)}), bf16[64,2,8,128]{3,2,1,0:T(8,128)(2,1)S(1)}, u32[]{:S(2)}, u32[]{:S(2)}) %all-to-all-start.7) | async-done | bytes 262176 | tf_op jit(solution)/shard_map/all_to_all | solution.py:106
  366.9 2.8 collective-permute-done.9
  (104 shorter events, 49.6 us)
Async XLA Ops:
  0.0 24.9 %copy-start.4 = (s32[24]{0:T(128)S(1)}, s32[24]{0:T(128)}, u32[]{:S(2)}) copy-start(s32[24]{0:T(128)} %param.15) | copy-start | bytes 292
  11.7 24.2 %all-to-all-start.2 = ((bf16[1,128,8,128]{3,2,0,1:T(8,128)(2,1)}), bf16[1,128,8,128]{3,2,0,1:T(8,128)(2,1)}, u32[]{:S(2)}, u32[]{:S(2)}) async-start(bf16[1,128,8,128]{3,2,0,1:T(8,128)(2,1)} %copy.151), calls=%async_computation.2 | async-start | bytes 524288 | tf_op jit(solution)/shard_map/all_to_all | solution.py:82
  28.7 16.6 %copy-start = (bf16[1,128,8,128]{3,1,2,0:T(8,128)(2,1)S(1)}, bf16[1,128,8,128]{3,1,2,0:T(8,128)(2,1)}, u32[]{:S(2)}) copy-start(bf16[1,128,8,128]{3,1,2,0:T(8,128)(2,1)} %get-tuple-element.96) | copy-start | bytes 786436
  30.1 33.1 %collective-permute-start = (bf16[3,128,2,1,512]{1,4,3,2,0:T(8,128)(2,1)S(1)}, bf16[3,128,2,1,512]{1,4,3,2,0:T(8,128)(2,1)}, u32[]{:S(2)}, u32[]{:S(2)}) collective-permute-start(bf16[3,128,2,1,512]{1,4,3,2,0:T(8,128)(2,1)S(1)} %get-tuple-element.89), channel_id=1, source_target_pairs={{0,1},{1,0},{2,3},{3,2},{4,5},{5,4},{6,7},{7,6},{8,9},{9,8},{10,11... | collective-permute-start | bytes 2359304 | tf_op jit(solution)/shard_map/ppermute | solution.py:19
  35.9 20.0 %all-to-all-start.4 = ((bf16[1,128,8,128]{3,2,0,1:T(8,128)(2,1)}), bf16[1,128,8,128]{3,2,0,1:T(8,128)(2,1)S(1)}, u32[]{:S(2)}, u32[]{:S(2)}) async-start(bf16[1,128,8,128]{3,2,0,1:T(8,128)(2,1)} %copy.155), calls=%async_computation.4 | async-start | bytes 524288 | tf_op jit(solution)/shard_map/all_to_all | solution.py:89
  55.9 18.3 %all-to-all-start = ((bf16[1,128,8,128]{3,2,0,1:T(8,128)(2,1)}), bf16[1,128,8,128]{3,2,0,1:T(8,128)(2,1)S(1)}, u32[]{:S(2)}, u32[]{:S(2)}) async-start(bf16[1,128,8,128]{3,2,0,1:T(8,128)(2,1)} %copy.147), calls=%async_computation | async-start | bytes 524288 | tf_op jit(solution)/shard_map/all_to_all | solution.py:96
  63.1 48.3 %copy-start.5 = (s32[128]{0:T(128)S(1)}, s32[128]{0:T(128)}, u32[]{:S(2)}) copy-start(s32[128]{0:T(128)} %param.17) | copy-start | bytes 1540
  63.2 48.9 %copy-start.3 = (s32[128,6]{0,1:T(8,128)S(1)}, s32[128,6]{0,1:T(8,128)}, u32[]{:S(2)}) copy-start(s32[128,6]{0,1:T(8,128)} %param.16) | copy-start | bytes 9220
  64.9 38.0 %collective-permute-start.1 = (bf16[3,128,1,2,512]{1,4,3,2,0:T(8,128)(2,1)S(1)}, bf16[3,128,1,2,512]{1,4,3,2,0:T(8,128)(2,1)S(1)}, u32[]{:S(2)}, u32[]{:S(2)}) collective-permute-start(bf16[3,128,1,2,512]{1,4,3,2,0:T(8,128)(2,1)S(1)} %get-tuple-element.87), channel_id=1, source_target_pairs={{0,2},{2,0},{1,3},{3,1},{4,6},{6,4},{5,7},{7,5},{8,10},{10,8},{9,1... | collective-permute-start | bytes 2359304 | tf_op jit(solution)/shard_map/ppermute | solution.py:19
  74.2 23.1 %all-to-all-start.3 = ((bf16[64,2,8,128]{3,1,0,2:T(2,128)(2,1)}), bf16[64,2,8,128]{3,1,0,2:T(2,128)(2,1)S(1)}, u32[]{:S(2)}, u32[]{:S(2)}) async-start(bf16[64,2,8,128]{3,1,0,2:T(2,128)(2,1)} %copy.152), calls=%async_computation.3 | async-start | bytes 524288 | tf_op jit(solution)/shard_map/all_to_all | solution.py:81
  97.3 19.1 %all-to-all-start.5 = ((bf16[64,2,8,128]{3,1,0,2:T(2,128)(2,1)}), bf16[64,2,8,128]{3,1,0,2:T(2,128)(2,1)S(1)}, u32[]{:S(2)}, u32[]{:S(2)}) async-start(bf16[64,2,8,128]{3,1,0,2:T(2,128)(2,1)} %copy.156), calls=%async_computation.5 | async-start | bytes 524288 | tf_op jit(solution)/shard_map/all_to_all | solution.py:88
  102.9 0.9 copy-start.1
  109.1 127.5 %collective-permute-start.2 = (bf16[2,512,512]{2,0,1:T(2,128)(2,1)S(1)}, bf16[2,512,512]{2,0,1:T(2,128)(2,1)}, u32[]{:S(2)}, u32[]{:S(2)}) collective-permute-start(bf16[2,512,512]{2,0,1:T(2,128)(2,1)S(1)} %bitcast.90), channel_id=1, source_target_pairs={{0,12},{1,13},{2,14},{3,15},{4,16},{5,17},{6,18},{7,19},{8,20},{9,... | collective-permute-start | bytes 3145736 | tf_op jit(solution)/shard_map/ppermute | solution.py:24
  112.3 128.5 %collective-permute-start.3 = (bf16[2,512,512]{2,0,1:T(2,128)(2,1)S(1)}, bf16[2,512,512]{2,0,1:T(2,128)(2,1)}, u32[]{:S(2)}, u32[]{:S(2)}) collective-permute-start(bf16[2,512,512]{2,0,1:T(2,128)(2,1)S(1)} %bitcast.91), channel_id=1, source_target_pairs={{0,8},{1,9},{2,10},{3,11},{4,12},{5,13},{6,14},{7,15},{8,16},{9,17... | collective-permute-start | bytes 3145736 | tf_op jit(solution)/shard_map/ppermute | solution.py:24
  116.4 111.2 %all-to-all-start.1 = ((bf16[64,2,8,128]{3,1,0,2:T(2,128)(2,1)}), bf16[64,2,8,128]{3,1,0,2:T(2,128)(2,1)S(1)}, u32[]{:S(2)}, u32[]{:S(2)}) async-start(bf16[64,2,8,128]{3,1,0,2:T(2,128)(2,1)} %copy.148), calls=%async_computation.1 | async-start | bytes 524288 | tf_op jit(solution)/shard_map/all_to_all | solution.py:95
  124.3 121.2 %collective-permute-start.4 = (bf16[2,512,512]{2,0,1:T(2,128)(2,1)S(1)}, bf16[2,512,512]{2,0,1:T(2,128)(2,1)}, u32[]{:S(2)}, u32[]{:S(2)}) collective-permute-start(bf16[2,512,512]{2,0,1:T(2,128)(2,1)S(1)} %bitcast.92), channel_id=1, source_target_pairs={{0,4},{1,5},{2,6},{3,7},{4,8},{5,9},{6,10},{7,11},{8,12},{9,13},{1... | collective-permute-start | bytes 3145736 | tf_op jit(solution)/shard_map/ppermute | solution.py:24
  128.6 119.8 %collective-permute-start.5 = (bf16[2,512,512]{2,0,1:T(2,128)(2,1)S(1)}, bf16[2,512,512]{2,0,1:T(2,128)(2,1)}, u32[]{:S(2)}, u32[]{:S(2)}) collective-permute-start(bf16[2,512,512]{2,0,1:T(2,128)(2,1)S(1)} %bitcast.93), channel_id=1, source_target_pairs={{0,508},{1,509},{2,510},{3,511},{4,0},{5,1},{6,2},{7,3},{8,4},{9,5... | collective-permute-start | bytes 3145736 | tf_op jit(solution)/shard_map/ppermute | solution.py:24
  230.1 113.4 %all-to-all-start.6 = ((bf16[512,2,1,128]{3,1,2,0:T(2,128)(2,1)}), bf16[512,2,1,128]{3,1,2,0:T(2,128)(2,1)S(1)}, u32[]{:S(2)}, u32[]{:S(2)}) async-start(bf16[512,2,1,128]{3,1,2,0:T(2,128)(2,1)} %bitcast.25), calls=%async_computation.6 | async-start | bytes 524288 | tf_op jit(solution)/shard_map/all_to_all | solution.py:107
  234.0 53.1 %collective-permute-start.7 = (bf16[2,512,512]{2,0,1:T(2,128)(2,1)S(1)}, bf16[2,512,512]{2,0,1:T(2,128)(2,1)}, u32[]{:S(2)}, u32[]{:S(2)}) collective-permute-start(bf16[2,512,512]{2,0,1:T(2,128)(2,1)S(1)} %bitcast.94), channel_id=1, source_target_pairs={{0,500},{1,501},{2,502},{3,503},{4,504},{5,505},{6,506},{7,507},{8... | collective-permute-start | bytes 3145736 | tf_op jit(solution)/shard_map/ppermute | solution.py:24
  236.7 49.7 %collective-permute-start.6 = (bf16[2,512,512]{2,0,1:T(2,128)(2,1)S(1)}, bf16[2,512,512]{2,0,1:T(2,128)(2,1)S(1)}, u32[]{:S(2)}, u32[]{:S(2)}) collective-permute-start(bf16[2,512,512]{2,0,1:T(2,128)(2,1)S(1)} %bitcast.95), channel_id=1, source_target_pairs={{0,504},{1,505},{2,506},{3,507},{4,508},{5,509},{6,510},{7,511},{8... | collective-permute-start | bytes 3145736 | tf_op jit(solution)/shard_map/ppermute | solution.py:24
  306.7 2.9 copy-start.2
  341.6 15.2 %collective-permute-start.8 = (bf16[128,2,1,512]{3,2,1,0:T(2,128)(2,1)S(1)}, bf16[128,2,1,512]{3,2,1,0:T(2,128)(2,1)S(1)}, u32[]{:S(2)}, u32[]{:S(2)}) collective-permute-start(bf16[128,2,1,512]{3,2,1,0:T(2,128)(2,1)S(1)} %get-tuple-element.93), channel_id=1, source_target_pairs={{0,1},{1,0},{2,3},{3,2},{4,5},{5,4},{6,7},{7,6},{8,9},{9,8},{10,11... | collective-permute-start | bytes 786440 | tf_op jit(solution)/shard_map/ppermute | solution.py:19
  344.5 22.2 %all-to-all-start.7 = ((bf16[64,2,8,128]{3,2,1,0:T(8,128)(2,1)}), bf16[64,2,8,128]{3,2,1,0:T(8,128)(2,1)S(1)}, u32[]{:S(2)}, u32[]{:S(2)}) async-start(bf16[64,2,8,128]{3,2,1,0:T(8,128)(2,1)} %copy.164), calls=%async_computation.7 | async-start | bytes 524288 | tf_op jit(solution)/shard_map/all_to_all | solution.py:106
  359.5 10.1 %collective-permute-start.9 = (bf16[128,1,2,512]{3,2,1,0:T(2,128)(2,1)S(1)}, bf16[128,1,2,512]{3,2,1,0:T(2,128)(2,1)S(1)}, u32[]{:S(2)}, u32[]{:S(2)}) collective-permute-start(bf16[128,1,2,512]{3,2,1,0:T(2,128)(2,1)S(1)} %get-tuple-element.91), channel_id=1, source_target_pairs={{0,2},{2,0},{1,3},{3,1},{4,6},{6,4},{5,7},{7,5},{8,10},{10,8},{9,1... | collective-permute-start | bytes 786440 | tf_op jit(solution)/shard_map/ppermute | solution.py:19
where the time goes:
time: 381 us; the launch traced here: 375 us
  waiting for transfers between devices  166 us (44%)
  starting transfers between devices  97.7 us (26%)
  local copies, waits for them, and re-layouts  66.2 us (17%)
  matrix products  23.3 us (6%)
  other arithmetic  18.3 us (5%)
    all_to_all x1, waiting for transfers between devices, local(): lax.all_to_all(lax.all_to_all(tv, 'seq', split_axis=1, concat_axis=0, til...  94.2 us
    ppermute x6, waiting for transfers between devices, from_behind(): lax.ppermute(array, axis, [(i, (i + by) % count) for i in range(count)])  38.8 us
    unnamed x23, local copies, waits for them, and re-layouts  24 us
    ppermute x6, starting transfers between devices, from_behind(): lax.ppermute(array, axis, [(i, (i + by) % count) for i in range(count)])  16.6 us
    all_to_all x1, starting transfers between devices, local(): lax.all_to_all(tq, 'seq', split_axis=1, concat_axis=0, tiled=True)  13.2 us
    all_to_all x1, starting transfers between devices, local(): lax.all_to_all(lax.all_to_all(tq, 'seq', split_axis=1, concat_axis=0, til...  12.9 us
    ppermute x4, starting transfers between devices, partner(): return lax.ppermute(block, axis, route)  11.8 us
    slice x1, local copies, waits for them, and re-layouts, local(): value_rows = stacked[:, 1].reshape(slot_total * positions, columns)  11.4 us
  transfers between devices with their start and end apart: 18, of which 10 were waited for; matrix products, arithmetic and copies ran while one was open for 24% of the time, Pallas kernels for 0%

commit v1 on v0

v1 whole, which is shorter than its diff:
```python
import functools
import math

import jax
import jax.numpy as jnp
from jax import lax
from jax.experimental import pallas as pl
from jax.experimental.pallas import tpu as pltpu
from jax.sharding import Mesh
from jax.sharding import PartitionSpec as P

HT = 8
W = 3
NB = 6
DEPTH = 128
LANES = 128
BF = jnp.bfloat16
F32 = jnp.float32
VMEM = pl.BlockSpec(memory_space=pltpu.VMEM)
SMEM = pl.BlockSpec(memory_space=pltpu.SMEM)
PARAMS = pltpu.CompilerParams(vmem_limit_bytes=40 * 1024 * 1024)


def columns_of(order_ref, slot):
    return pl.ds(pl.multiple_of(order_ref[slot] * DEPTH, DEPTH), DEPTH)


def pack_spatial_kernel(order_ref, *refs):
    half = len(refs) // 2
    for src, dst in zip(refs[:half], refs[half:]):
        for dest in range(dst.shape[0]):
            for head in range(dst.shape[1]):
                slot = HT + dest * dst.shape[1] + head
                dst[dest, head] = src[:, columns_of(order_ref, slot)]


def pack_spatial(order, arrays, dests, heads):
    rows = arrays[0].shape[0]
    out = jax.ShapeDtypeStruct((dests, heads, rows, DEPTH), BF)
    return pl.pallas_call(
        pack_spatial_kernel,
        out_shape=[out] * len(arrays),
        in_specs=[SMEM] + [VMEM] * len(arrays),
        out_specs=[VMEM] * len(arrays),
        compiler_params=PARAMS,
    )(order, *arrays)


def pack_temporal_kernel(items, order_ref, q_ref, k_ref, v_ref, out_ref):
    pieces = q_ref.shape[0] // items
    for which, src in enumerate((q_ref, k_ref, v_ref)):
        for head in range(HT):
            block = src[:, columns_of(order_ref, head)]
            out_ref[head * pieces : (head + 1) * pieces, which] = block.reshape(pieces, items, DEPTH)


def pack_temporal(order, q, k, v, items):
    dests = HT * q.shape[0] // items
    return pl.pallas_call(
        functools.partial(pack_temporal_kernel, items),
        out_shape=jax.ShapeDtypeStruct((dests, 3, items, DEPTH), BF),
        in_specs=[SMEM] + [VMEM] * 3,
        out_specs=VMEM,
        compiler_params=PARAMS,
    )(order, q, k, v)


def temporal_kernel(in_ref, out_ref):
    frames, _, items, depth = in_ref.shape
    total = frames * items
    step = 256
    factor = depth ** (-0.5) * math.log2(math.e)
    k = in_ref[:, 1].reshape(total, depth)
    v = in_ref[:, 2].reshape(total, depth)
    row_item = lax.broadcasted_iota(jnp.int32, (step, total), 0) % items
    col_item = lax.broadcasted_iota(jnp.int32, (step, total), 1) % items
    same = row_item == col_item
    per = step // items
    for at in range(frames // per):
        q = in_ref[at * per : (at + 1) * per, 0].reshape(step, depth)
        s = lax.dot_general(q, k, (((1,), (1,)), ((), ())), preferred_element_type=F32)
        s = jnp.where(same, s * factor, -jnp.inf)
        p = jnp.exp2(s - jnp.max(s, axis=1, keepdims=True))
        total_p = jnp.sum(p, axis=1, keepdims=True)
        o = jnp.dot(p.astype(BF), v, preferred_element_type=F32) / total_p
        out_ref[at * per : (at + 1) * per] = o.astype(BF).reshape(per, items, depth)


def temporal_attend(arrived):
    frames, _, items, depth = arrived.shape
    return pl.pallas_call(
        temporal_kernel,
        out_shape=jax.ShapeDtypeStruct((frames, items, depth), BF),
        in_specs=[VMEM],
        out_specs=VMEM,
        compiler_params=PARAMS,
    )(arrived)


def spatial_kernel(frames, base_ref, kb_ref, bc_ref, q_ref, *refs):
    (k0, v0, km1, vm1, kp1, vp1, km2, vm2, kp2, vp2, o_ref, m_ref, l_ref, acc_ref) = refs
    pieces = q_ref.shape[0] // 2
    rows, depth = q_ref.shape[2:]
    size = pieces * rows
    factor = depth ** (-0.5) * math.log2(math.e)
    base = base_ref[0]
    slots = {
        -3: (km2, vm2, 0),
        -2: (km1, vm1, 0),
        -1: (km1, vm1, pieces),
        0: (k0, v0, 0),
        1: (k0, v0, pieces),
        2: (kp1, vp1, 0),
        3: (kp1, vp1, pieces),
        4: (kp2, vp2, 0),
    }
    heads = q_ref.shape[1]
    for mine in range(2):
        frame = base + mine
        count = bc_ref[frame]
        listed = [kb_ref[frame, n] for n in range(NB)]

        def used(slot):
            target = lax.rem(base + slot + frames, frames)
            hit = (listed[0] == target) & (count > 0)
            for n in range(1, NB):
                hit = hit | ((listed[n] == target) & (count > n))
            return hit

        for head in range(heads):
            q = q_ref[mine * pieces : (mine + 1) * pieces, head].reshape(size, depth)

            def scores(slot):
                k_ref, _, at = slots[slot]
                k = k_ref[at : at + pieces, head].reshape(size, depth)
                return lax.dot_general(
                    q, k, (((1,), (1,)), ((), ())), preferred_element_type=F32
                )

            def value(slot):
                _, v_ref, at = slots[slot]
                return v_ref[at : at + pieces, head].reshape(size, depth)

            s = scores(mine) * factor
            top = jnp.max(s, axis=1, keepdims=True)
            p = jnp.exp2(s - top)
            m_ref[...] = jnp.broadcast_to(top, m_ref.shape)
            l_ref[...] = jnp.broadcast_to(jnp.sum(p, axis=1, keepdims=True), l_ref.shape)
            acc_ref[...] = jnp.dot(p.astype(BF), value(mine), preferred_element_type=F32)
            for reach in range(-W, W + 1):
                if reach == 0:
                    continue
                slot = mine + reach

                @pl.when(used(slot))
                def _():
                    s = scores(slot) * factor
                    old = m_ref[...]
                    new = jnp.maximum(old, jnp.max(s, axis=1, keepdims=True))
                    p = jnp.exp2(s - new[:, :1])
                    alpha = jnp.exp2(old - new)
                    m_ref[...] = new
                    l_ref[...] = l_ref[...] * alpha + jnp.sum(p, axis=1, keepdims=True)
                    acc_ref[...] = acc_ref[...] * alpha + jnp.dot(
                        p.astype(BF), value(slot), preferred_element_type=F32
                    )

            o = (acc_ref[...] / l_ref[...]).astype(BF)
            o_ref[mine * pieces : (mine + 1) * pieces, head] = o.reshape(pieces, rows, depth)


def spatial_attend(base, kb, bc, q, parts, frames):
    size = q.shape[0] // 2 * q.shape[2]
    return pl.pallas_call(
        functools.partial(spatial_kernel, frames),
        out_shape=jax.ShapeDtypeStruct(q.shape, BF),
        in_specs=[SMEM] * 3 + [VMEM] * (1 + len(parts)),
        out_specs=VMEM,
        scratch_shapes=[
            pltpu.VMEM((size, LANES), F32),
            pltpu.VMEM((size, LANES), F32),
            pltpu.VMEM((size, DEPTH), F32),
        ],
        compiler_params=PARAMS,
    )(base, kb, bc, q, *parts)


def assemble_kernel(order_ref, t_ref, s_ref, out_ref):
    rows = out_ref.shape[0]
    pieces = t_ref.shape[0] // HT
    for head in range(HT):
        block = t_ref[head * pieces : (head + 1) * pieces].reshape(rows, DEPTH)
        out_ref[:, columns_of(order_ref, head)] = block
    for dest in range(s_ref.shape[0]):
        for head in range(s_ref.shape[1]):
            slot = HT + dest * s_ref.shape[1] + head
            out_ref[:, columns_of(order_ref, slot)] = s_ref[dest, head]


def assemble(order, temporal, spatial, rows, width):
    return pl.pallas_call(
        assemble_kernel,
        out_shape=jax.ShapeDtypeStruct((rows, width), BF),
        in_specs=[SMEM, VMEM, VMEM],
        out_specs=VMEM,
        compiler_params=PARAMS,
    )(order, temporal, spatial)


def exchange(array, axes):
    return lax.all_to_all(array, axes, 0, 0, tiled=True)


def from_block(array, by):
    count = lax.axis_size("grp") * lax.axis_size("y")
    return lax.ppermute(array, ("grp", "y"), [((i + by) % count, i) for i in range(count)])


def local(queries, keys, values, head_order, key_blocks, block_count):
    rows, width = queries.shape
    heads = width // DEPTH
    quarters = lax.axis_size("x")
    frames = lax.axis_size("grp") * lax.axis_size("y") * 2
    dests = 2 * quarters
    share = (heads - HT) // dests
    items = HT * rows // frames
    base = (lax.axis_index("grp") * lax.axis_size("y") + lax.axis_index("y")) * 2
    base = base.astype(jnp.int32).reshape(1)

    sk, sv = pack_spatial(head_order, (keys, values), dests, share)
    k0 = exchange(sk, ("zl", "x"))
    v0 = exchange(sv, ("zl", "x"))
    (sq,) = pack_spatial(head_order, (queries,), dests, share)
    st = pack_temporal(head_order, queries, keys, values, items)
    kp1, vp1 = from_block(k0, 1), from_block(v0, 1)
    km1, vm1 = from_block(k0, -1), from_block(v0, -1)
    kp2, vp2 = from_block(k0[:quarters], 2), from_block(v0[:quarters], 2)
    km2, vm2 = from_block(k0[quarters:], -2), from_block(v0[quarters:], -2)
    at = exchange(st, ("grp", "y", "zl"))
    q0 = exchange(sq, ("zl", "x"))
    to = temporal_attend(at)
    tr = exchange(to, ("grp", "y", "zl"))
    so = spatial_attend(
        base, key_blocks, block_count, q0,
        (k0, v0, km1, vm1, kp1, vp1, km2, vm2, kp2, vp2), frames,
    )
    sr = exchange(so, ("zl", "x"))
    return assemble(head_order, tr, sr, rows, width)


def solution(mesh):
    grp, seq = mesh.shape["grp"], mesh.shape["seq"]
    fine = Mesh(mesh.devices.reshape(grp, seq // 8, 2, 4), ("grp", "y", "zl", "x"))
    tokens = P(("grp", "y", "zl", "x"), None)
    return jax.shard_map(
        local,
        mesh=fine,
        in_specs=(tokens, tokens, tokens, P(), P(), P()),
        out_specs=tokens,
        check_vma=False,
    )
```

time: 381 us -> 185 us (0.49)
  the two profiles are of different devices: /device:TPU:1 before, /device:TPU:48 now
where the time goes in v1:
time: 185 us; the launch traced here: 184 us
  starting transfers between devices  67 us (36%)
  waiting for transfers between devices  44.9 us (24%)
  blocking collectives  31.5 us (17%)
  Pallas kernels  28.9 us (16%)
  local copies, waits for them, and re-layouts  11.1 us (6%)
    ppermute x8, starting transfers between devices, from_block(): lax.ppermute(array, ('grp', 'y'), [((i + by) % count, i) for i in range(c...  33.8 us
    all_to_all x4, starting transfers between devices, exchange(): return lax.all_to_all(array, axes, 0, 0, tiled=True)  33.2 us
    all_to_all x2, blocking collectives, exchange(): return lax.all_to_all(array, axes, 0, 0, tiled=True)  31.5 us
    all_to_all x4, waiting for transfers between devices, exchange(): return lax.all_to_all(array, axes, 0, 0, tiled=True)  28.8 us
    pallas_call x1, Pallas kernels, spatial_attend(): pl.pallas_call(functools.partial(spatial_kernel, frames), out_shape=jax.S...  21.4 us
    ppermute x8, waiting for transfers between devices, from_block(): lax.ppermute(array, ('grp', 'y'), [((i + by) % count, i) for i in range(c...  16.2 us
    unnamed x37, local copies, waits for them, and re-layouts  9.55 us
  transfers between devices with their start and end apart: 12, of which 4 were waited for; matrix products, arithmetic and copies ran while one was open for 1% of the time, Pallas kernels for 14%

profile of v1, /device:TPU:48, one launch (start us, length us, event | category | flops | bytes accessed | tf_op | source)
XLA Modules:
  0.0 183.6 jit_solution(10787079246323128140)
XLA Ops:
  0.0 1.1 copy-done
  1.1 1.1 copy-done.2
  2.3 0.7 copy-done.13
  2.9 0.8 shard_map.67
  3.8 0.0 copy-start.3
  3.8 16.1 %all_to_all.30.refs_0_ = bf16[8,2,128,128]{3,2,1,0:T(8,128)(2,1)S(1)} all-to-all(bf16[8,2,128,128]{3,2,1,0:T(8,128)(2,1)S(1)} %get-tuple-element.7), channel_id=1, replica_groups=mesh['grp'=8,'y'=8,'zl'=2,'x'=4] {'zl','x'}, dimensions={0} | all-to-all | bytes 1048576 | tf_op jit(solution)/shard_map/all_to_all | solution.py:211
  19.9 3.6 %all-to-all-start.4 = ((bf16[8,2,128,128]{3,2,1,0:T(8,128)(2,1)}), bf16[8,2,128,128]{3,2,1,0:T(8,128)(2,1)S(1)}, u32[]{:S(2)}, u32[]{:S(2)}) async-start(bf16[8,2,128,128]{3,2,1,0:T(8,128)(2,1)} %copy-done.6), calls=%async_computation.4 | async-start | bytes 1048576 | tf_op jit(solution)/shard_map/all_to_all | solution.py:211
  23.6 0.8 shard_map.64
  24.3 0.0 copy-start.5
  24.3 0.9 copy-done.5
  25.2 6.5 %all-to-all-done.4.refs_1_ = bf16[8,2,128,128]{3,2,1,0:T(8,128)(2,1)S(1)} async-done(((bf16[8,2,128,128]{3,2,1,0:T(8,128)(2,1)}), bf16[8,2,128,128]{3,2,1,0:T(8,128)(2,1)S(1)}, u32[]{:S(2)}, u32[]{:S(2)}) %all-to-all-start.4) | async-done | bytes 524320 | tf_op jit(solution)/shard_map/all_to_all | solution.py:211
  31.7 15.9 %all-to-all-start = ((bf16[128,3,8,128]{3,2,1,0:T(8,128)(2,1)}), bf16[128,3,8,128]{3,2,1,0:T(8,128)(2,1)S(1)}, u32[]{:S(2)}, u32[]{:S(2)}) async-start(bf16[128,3,8,128]{3,2,1,0:T(8,128)(2,1)} %copy-done.5), calls=%async_computation | async-start | bytes 1572864 | tf_op jit(solution)/shard_map/all_to_all | solution.py:211
  47.6 1.5 shard_map.66
  49.1 22.2 %all-to-all-done.in_ref = bf16[128,3,8,128]{3,2,1,0:T(8,128)(2,1)S(1)} async-done(((bf16[128,3,8,128]{3,2,1,0:T(8,128)(2,1)}), bf16[128,3,8,128]{3,2,1,0:T(8,128)(2,1)S(1)}, u32[]{:S(2)}, u32[]{:S(2)}) %all-to-all-start) | async-done | bytes 786464 | tf_op jit(solution)/shard_map/all_to_all | solution.py:211
  71.3 3.5 %all-to-all-start.2 = ((bf16[8,2,128,128]{3,2,1,0:T(8,128)(2,1)}), bf16[8,2,128,128]{3,2,1,0:T(8,128)(2,1)S(1)}, u32[]{:S(2)}, u32[]{:S(2)}) async-start(bf16[8,2,128,128]{3,2,1,0:T(8,128)(2,1)} %shard_map.66), calls=%async_computation.2 | async-start | bytes 1048576 | tf_op jit(solution)/shard_map/all_to_all | solution.py:211
  74.8 0.7 fusion.1
  75.6 2.8 %collective-permute-start.4 = (bf16[4,2,128,128]{3,2,1,0:T(8,128)(2,1)S(1)}, bf16[4,2,128,128]{3,2,1,0:T(8,128)(2,1)S(1)}, u32[]{:S(2)}, u32[]{:S(2)}) collective-permute-start(bf16[4,2,128,128]{3,2,1,0:T(8,128)(2,1)S(1)} %get-tuple-element.12), channel_id=1, source_target_pairs={{496,0},{504,8},{0,16},{8,24},{16,32},{24,40},{32,48},{40,56},{48,... | collective-permute-start | bytes 786440 | tf_op jit(solution)/shard_map/ppermute | solution.py:216
  78.4 0.8 fusion
  79.2 3.8 %collective-permute-start.5 = (bf16[4,2,128,128]{3,2,1,0:T(8,128)(2,1)S(1)}, bf16[4,2,128,128]{3,2,1,0:T(8,128)(2,1)S(1)}, u32[]{:S(2)}, u32[]{:S(2)}) collective-permute-start(bf16[4,2,128,128]{3,2,1,0:T(8,128)(2,1)S(1)} %get-tuple-element.10), channel_id=1, source_target_pairs={{496,0},{504,8},{0,16},{8,24},{16,32},{24,40},{32,48},{40,56},{48,... | collective-permute-start | bytes 786440 | tf_op jit(solution)/shard_map/ppermute | solution.py:216
  83.0 2.9 %collective-permute-start.6 = (bf16[4,2,128,128]{3,2,1,0:T(8,128)(2,1)}, bf16[4,2,128,128]{3,2,1,0:T(8,128)(2,1)}, u32[]{:S(2)}, u32[]{:S(2)}) collective-permute-start(bf16[4,2,128,128]{3,2,1,0:T(8,128)(2,1)} %get-tuple-element.11), channel_id=1, source_target_pairs={{16,0},{24,8},{32,16},{40,24},{48,32},{56,40},{64,48},{72,56},{80,... | collective-permute-start | bytes 786440 | tf_op jit(solution)/shard_map/ppermute | solution.py:216
  85.9 4.0 %collective-permute-start = (bf16[8,2,128,128]{3,2,1,0:T(8,128)(2,1)S(1)}, bf16[8,2,128,128]{3,2,1,0:T(8,128)(2,1)S(1)}, u32[]{:S(2)}, u32[]{:S(2)}) collective-permute-start(bf16[8,2,128,128]{3,2,1,0:T(8,128)(2,1)S(1)} %all_to_all.30.refs_0_), channel_id=1, source_target_pairs={{504,0},{0,8},{8,16},{16,24},{24,32},{32,40},{40,48},{48,56},{56,6... | collective-permute-start | bytes 1572872 | tf_op jit(solution)/shard_map/ppermute | solution.py:216
  89.9 3.2 %collective-permute-start.1 = (bf16[8,2,128,128]{3,2,1,0:T(8,128)(2,1)S(1)}, bf16[8,2,128,128]{3,2,1,0:T(8,128)(2,1)S(1)}, u32[]{:S(2)}, u32[]{:S(2)}) collective-permute-start(bf16[8,2,128,128]{3,2,1,0:T(8,128)(2,1)S(1)} %all-to-all-done.4.refs_1_), channel_id=1, source_target_pairs={{504,0},{0,8},{8,16},{16,24},{24,32},{32,40},{40,48},{48,56},{56,6... | collective-permute-start | bytes 1572872 | tf_op jit(solution)/shard_map/ppermute | solution.py:216
  93.2 0.0 collective-permute-done.4.refs_6_
  93.2 0.7 copy-done.7
  93.9 7.1 %collective-permute-start.2 = (bf16[8,2,128,128]{3,2,1,0:T(8,128)(2,1)S(1)}, bf16[8,2,128,128]{3,2,1,0:T(8,128)(2,1)}, u32[]{:S(2)}, u32[]{:S(2)}) collective-permute-start(bf16[8,2,128,128]{3,2,1,0:T(8,128)(2,1)S(1)} %all_to_all.30.refs_0_), channel_id=1, source_target_pairs={{8,0},{16,8},{24,16},{32,24},{40,32},{48,40},{56,48},{64,56},{72,6... | collective-permute-start | bytes 1572872 | tf_op jit(solution)/shard_map/ppermute | solution.py:216
  101.0 1.7 collective-permute-done.5.refs_7_
  102.7 0.7 copy-done.9
  103.4 5.6 %collective-permute-start.3 = (bf16[8,2,128,128]{3,2,1,0:T(8,128)(2,1)S(1)}, bf16[8,2,128,128]{3,2,1,0:T(8,128)(2,1)}, u32[]{:S(2)}, u32[]{:S(2)}) collective-permute-start(bf16[8,2,128,128]{3,2,1,0:T(8,128)(2,1)S(1)} %all-to-all-done.4.refs_1_), channel_id=1, source_target_pairs={{8,0},{16,8},{24,16},{32,24},{40,32},{48,40},{56,48},{64,56},{72,6... | collective-permute-start | bytes 1572872 | tf_op jit(solution)/shard_map/ppermute | solution.py:216
  109.0 2.8 %shard_map.65 = bf16[128,8,128]{2,1,0:T(8,128)(2,1)} custom-call(bf16[128,3,8,128]{3,2,1,0:T(8,128)(2,1)S(1)} %all-to-all-done.in_ref), custom_call_target="tpu_custom_call" | custom-call | tf_op jit(solution)/shard_map/pallas_call | solution.py:91
  111.9 0.0 all-to-all-done.2.q_ref
  111.9 10.2 %all-to-all-start.1 = ((bf16[128,8,128]{2,1,0:T(8,128)(2,1)}), bf16[128,8,128]{2,1,0:T(8,128)(2,1)S(1)}, u32[]{:S(2)}, u32[]{:S(2)}) async-start(bf16[128,8,128]{2,1,0:T(8,128)(2,1)} %shard_map.65), calls=%async_computation.1 | async-start | bytes 524288 | tf_op jit(solution)/shard_map/all_to_all | solution.py:211
  122.1 4.3 %collective-permute-start.7 = (bf16[4,2,128,128]{3,2,1,0:T(8,128)(2,1)S(1)}, bf16[4,2,128,128]{3,2,1,0:T(8,128)(2,1)S(1)}, u32[]{:S(2)}, u32[]{:S(2)}) collective-permute-start(bf16[4,2,128,128]{3,2,1,0:T(8,128)(2,1)S(1)} %copy-done.16), channel_id=1, source_target_pairs={{16,0},{24,8},{32,16},{40,24},{48,32},{56,40},{64,48},{72,56},{80,... | collective-permute-start | bytes 786440 | tf_op jit(solution)/shard_map/ppermute | solution.py:216
  126.4 0.0 copy-start.17
  126.4 0.7 copy-done.17
  127.1 0.1 copy.7.kb_ref
  127.2 0.0 copy-start.15
  127.2 14.4 %collective-permute-done.7.refs_9_ = bf16[4,2,128,128]{3,2,1,0:T(8,128)(2,1)S(1)} collective-permute-done((bf16[4,2,128,128]{3,2,1,0:T(8,128)(2,1)S(1)}, bf16[4,2,128,128]{3,2,1,0:T(8,128)(2,1)S(1)}, u32[]{:S(2)}, u32[]{:S(2)}) %collective-permute-start.7) | collective-permute-done | bytes 262176 | tf_op jit(solution)/shard_map/ppermute | solution.py:216
  141.7 0.7 copy-done.11
  142.4 0.0 collective-permute-done.refs_2_
  142.4 0.0 collective-permute-done.1.refs_3_
  142.4 0.0 collective-permute-done.2.refs_4_
  142.4 0.9 copy-done.8
  143.4 0.9 copy-done.10
  144.3 0.9 copy-done.12
  145.3 21.4 %shard_map.68 = bf16[8,2,128,128]{3,2,1,0:T(8,128)(2,1)S(1)} custom-call(s32[1]{0:T(128)} %bitcast.base_ref, s32[128,6]{1,0:T(8,128)S(1)} %copy.7.kb_ref, s32[128]{0:T(128)S(1)} %copy-done.15, bf16[8,2,128,128]{3,2,1,0:T(8,128)(2,1)S(1)} %all-to-all-done.2.q_ref, bf16[8,2,128,128]{3,2,1,0:T(8,128)(2,1)S(1)} %all_to_all.30.refs_0_, ...), custom_call_target="tpu_custom_call" | custom-call | tf_op jit(solution)/shard_map/pallas_call | solution.py:174
  166.6 0.0 all-to-all-done.1.t_ref
  166.7 15.4 %all_to_all.31.s_ref = bf16[8,2,128,128]{3,2,1,0:T(8,128)(2,1)S(1)} all-to-all(bf16[8,2,128,128]{3,2,1,0:T(8,128)(2,1)S(1)} %shard_map.68), channel_id=1, replica_groups=mesh['grp'=8,'y'=8,'zl'=2,'x'=4] {'zl','x'}, dimensions={0} | all-to-all | bytes 1048576 | tf_op jit(solution)/shard_map/all_to_all | solution.py:211
  182.0 1.6 shard_map.69
  (23 shorter events, 0.0 us)
Async XLA Ops:
  0.0 1.1 copy-start
  1.1 1.1 copy-start.2
  2.3 0.7 copy-start.13
  2.9 20.6 %copy-start.4 = (bf16[128,3072]{1,0:T(8,128)(2,1)S(1)}, bf16[128,3072]{1,0:T(8,128)(2,1)}, u32[]{:S(2)}) copy-start(bf16[128,3072]{1,0:T(8,128)(2,1)} %refs_0_.2) | copy-start | bytes 2359300
  3.7 16.1 %copy-start.6 = (bf16[8,2,128,128]{3,2,1,0:T(8,128)(2,1)}, bf16[8,2,128,128]{3,2,1,0:T(8,128)(2,1)S(1)}, u32[]{:S(2)}) copy-start(bf16[8,2,128,128]{3,2,1,0:T(8,128)(2,1)S(1)} %get-tuple-element.8) | copy-start | bytes 1572868
  3.8 19.8 %copy-start.3 = (bf16[128,3072]{1,0:T(8,128)(2,1)S(1)}, bf16[128,3072]{1,0:T(8,128)(2,1)}, u32[]{:S(2)}) copy-start(bf16[128,3072]{1,0:T(8,128)(2,1)} %refs_1_.1) | copy-start | bytes 2359300
  19.9 3.7 %copy-start.1 = (bf16[128,3072]{1,0:T(8,128)(2,1)S(1)}, bf16[128,3072]{1,0:T(8,128)(2,1)}, u32[]{:S(2)}) copy-start(bf16[128,3072]{1,0:T(8,128)(2,1)} %refs_0_.3) | copy-start | bytes 2359300
  19.9 3.7 %copy-start.14 = (s32[24]{0:T(128)S(1)}, s32[24]{0:T(128)}, u32[]{:S(2)}) copy-start(s32[24]{0:T(128)} %order_ref.7) | copy-start | bytes 292
  19.9 11.8 %all-to-all-start.4 = ((bf16[8,2,128,128]{3,2,1,0:T(8,128)(2,1)}), bf16[8,2,128,128]{3,2,1,0:T(8,128)(2,1)S(1)}, u32[]{:S(2)}, u32[]{:S(2)}) async-start(bf16[8,2,128,128]{3,2,1,0:T(8,128)(2,1)} %copy-done.6), calls=%async_computation.4 | async-start | bytes 1048576 | tf_op jit(solution)/shard_map/all_to_all | solution.py:211
  24.3 0.9 copy-start.5
  31.7 39.6 %all-to-all-start = ((bf16[128,3,8,128]{3,2,1,0:T(8,128)(2,1)}), bf16[128,3,8,128]{3,2,1,0:T(8,128)(2,1)S(1)}, u32[]{:S(2)}, u32[]{:S(2)}) async-start(bf16[128,3,8,128]{3,2,1,0:T(8,128)(2,1)} %copy-done.5), calls=%async_computation | async-start | bytes 1572864 | tf_op jit(solution)/shard_map/all_to_all | solution.py:211
  71.3 40.5 %all-to-all-start.2 = ((bf16[8,2,128,128]{3,2,1,0:T(8,128)(2,1)}), bf16[8,2,128,128]{3,2,1,0:T(8,128)(2,1)S(1)}, u32[]{:S(2)}, u32[]{:S(2)}) async-start(bf16[8,2,128,128]{3,2,1,0:T(8,128)(2,1)} %shard_map.66), calls=%async_computation.2 | async-start | bytes 1048576 | tf_op jit(solution)/shard_map/all_to_all | solution.py:211
  75.6 17.6 %collective-permute-start.4 = (bf16[4,2,128,128]{3,2,1,0:T(8,128)(2,1)S(1)}, bf16[4,2,128,128]{3,2,1,0:T(8,128)(2,1)S(1)}, u32[]{:S(2)}, u32[]{:S(2)}) collective-permute-start(bf16[4,2,128,128]{3,2,1,0:T(8,128)(2,1)S(1)} %get-tuple-element.12), channel_id=1, source_target_pairs={{496,0},{504,8},{0,16},{8,24},{16,32},{24,40},{32,48},{40,56},{48,... | collective-permute-start | bytes 786440 | tf_op jit(solution)/shard_map/ppermute | solution.py:216
  79.2 23.6 %collective-permute-start.5 = (bf16[4,2,128,128]{3,2,1,0:T(8,128)(2,1)S(1)}, bf16[4,2,128,128]{3,2,1,0:T(8,128)(2,1)S(1)}, u32[]{:S(2)}, u32[]{:S(2)}) collective-permute-start(bf16[4,2,128,128]{3,2,1,0:T(8,128)(2,1)S(1)} %get-tuple-element.10), channel_id=1, source_target_pairs={{496,0},{504,8},{0,16},{8,24},{16,32},{24,40},{32,48},{40,56},{48,... | collective-permute-start | bytes 786440 | tf_op jit(solution)/shard_map/ppermute | solution.py:216
  83.0 39.1 %collective-permute-start.6 = (bf16[4,2,128,128]{3,2,1,0:T(8,128)(2,1)}, bf16[4,2,128,128]{3,2,1,0:T(8,128)(2,1)}, u32[]{:S(2)}, u32[]{:S(2)}) collective-permute-start(bf16[4,2,128,128]{3,2,1,0:T(8,128)(2,1)} %get-tuple-element.11), channel_id=1, source_target_pairs={{16,0},{24,8},{32,16},{40,24},{48,32},{56,40},{64,48},{72,56},{80,... | collective-permute-start | bytes 786440 | tf_op jit(solution)/shard_map/ppermute | solution.py:216
  85.9 56.5 %collective-permute-start = (bf16[8,2,128,128]{3,2,1,0:T(8,128)(2,1)S(1)}, bf16[8,2,128,128]{3,2,1,0:T(8,128)(2,1)S(1)}, u32[]{:S(2)}, u32[]{:S(2)}) collective-permute-start(bf16[8,2,128,128]{3,2,1,0:T(8,128)(2,1)S(1)} %all_to_all.30.refs_0_), channel_id=1, source_target_pairs={{504,0},{0,8},{8,16},{16,24},{24,32},{32,40},{40,48},{48,56},{56,6... | collective-permute-start | bytes 1572872 | tf_op jit(solution)/shard_map/ppermute | solution.py:216
  89.9 52.5 %collective-permute-start.1 = (bf16[8,2,128,128]{3,2,1,0:T(8,128)(2,1)S(1)}, bf16[8,2,128,128]{3,2,1,0:T(8,128)(2,1)S(1)}, u32[]{:S(2)}, u32[]{:S(2)}) collective-permute-start(bf16[8,2,128,128]{3,2,1,0:T(8,128)(2,1)S(1)} %all-to-all-done.4.refs_1_), channel_id=1, source_target_pairs={{504,0},{0,8},{8,16},{16,24},{24,32},{32,40},{40,48},{48,56},{56,6... | collective-permute-start | bytes 1572872 | tf_op jit(solution)/shard_map/ppermute | solution.py:216
  93.2 0.7 copy-start.7
  93.9 48.5 %collective-permute-start.2 = (bf16[8,2,128,128]{3,2,1,0:T(8,128)(2,1)S(1)}, bf16[8,2,128,128]{3,2,1,0:T(8,128)(2,1)}, u32[]{:S(2)}, u32[]{:S(2)}) collective-permute-start(bf16[8,2,128,128]{3,2,1,0:T(8,128)(2,1)S(1)} %all_to_all.30.refs_0_), channel_id=1, source_target_pairs={{8,0},{16,8},{24,16},{32,24},{40,32},{48,40},{56,48},{64,56},{72,6... | collective-permute-start | bytes 1572872 | tf_op jit(solution)/shard_map/ppermute | solution.py:216
  102.7 0.7 copy-start.9
  103.4 39.0 %collective-permute-start.3 = (bf16[8,2,128,128]{3,2,1,0:T(8,128)(2,1)S(1)}, bf16[8,2,128,128]{3,2,1,0:T(8,128)(2,1)}, u32[]{:S(2)}, u32[]{:S(2)}) collective-permute-start(bf16[8,2,128,128]{3,2,1,0:T(8,128)(2,1)S(1)} %all-to-all-done.4.refs_1_), channel_id=1, source_target_pairs={{8,0},{16,8},{24,16},{32,24},{40,32},{48,40},{56,48},{64,56},{72,6... | collective-permute-start | bytes 1572872 | tf_op jit(solution)/shard_map/ppermute | solution.py:216
  111.9 10.3 %copy-start.16 = (bf16[4,2,128,128]{3,2,1,0:T(8,128)(2,1)S(1)}, bf16[4,2,128,128]{3,2,1,0:T(8,128)(2,1)}, u32[]{:S(2)}) copy-start(bf16[4,2,128,128]{3,2,1,0:T(8,128)(2,1)} %get-tuple-element.9) | copy-start | bytes 786436
  111.9 54.8 %all-to-all-start.1 = ((bf16[128,8,128]{2,1,0:T(8,128)(2,1)}), bf16[128,8,128]{2,1,0:T(8,128)(2,1)S(1)}, u32[]{:S(2)}, u32[]{:S(2)}) async-start(bf16[128,8,128]{2,1,0:T(8,128)(2,1)} %shard_map.65), calls=%async_computation.1 | async-start | bytes 524288 | tf_op jit(solution)/shard_map/all_to_all | solution.py:211
  122.1 19.5 %collective-permute-start.7 = (bf16[4,2,128,128]{3,2,1,0:T(8,128)(2,1)S(1)}, bf16[4,2,128,128]{3,2,1,0:T(8,128)(2,1)S(1)}, u32[]{:S(2)}, u32[]{:S(2)}) collective-permute-start(bf16[4,2,128,128]{3,2,1,0:T(8,128)(2,1)S(1)} %copy-done.16), channel_id=1, source_target_pairs={{16,0},{24,8},{32,16},{40,24},{48,32},{56,40},{64,48},{72,56},{80,... | collective-permute-start | bytes 786440 | tf_op jit(solution)/shard_map/ppermute | solution.py:216
  126.4 0.7 copy-start.17
  127.2 15.2 %copy-start.15 = (s32[128]{0:T(128)S(1)}, s32[128]{0:T(128)}, u32[]{:S(2)}) copy-start(s32[128]{0:T(128)} %bc_ref.1) | copy-start | bytes 1540
  141.7 0.7 copy-start.11
  142.4 1.0 copy-start.8
  143.4 0.9 copy-start.10
  144.3 0.9 copy-start.12

commit v2 on v1

--- a/solution.py
+++ b/solution.py
@@ -26,22 +26,21 @@
 
 
 def pack_spatial_kernel(order_ref, *refs):
-    half = len(refs) // 2
-    for src, dst in zip(refs[:half], refs[half:]):
+    dst = refs[-1]
+    for which, src in enumerate(refs[:-1]):
         for dest in range(dst.shape[0]):
-            for head in range(dst.shape[1]):
-                slot = HT + dest * dst.shape[1] + head
-                dst[dest, head] = src[:, columns_of(order_ref, slot)]
+            for head in range(dst.shape[2]):
+                slot = HT + dest * dst.shape[2] + head
+                dst[dest, which, head] = src[:, columns_of(order_ref, slot)]
 
 
 def pack_spatial(order, arrays, dests, heads):
     rows = arrays[0].shape[0]
-    out = jax.ShapeDtypeStruct((dests, heads, rows, DEPTH), BF)
     return pl.pallas_call(
         pack_spatial_kernel,
-        out_shape=[out] * len(arrays),
+        out_shape=jax.ShapeDtypeStruct((dests, len(arrays), heads, rows, DEPTH), BF),
         in_specs=[SMEM] + [VMEM] * len(arrays),
-        out_specs=[VMEM] * len(arrays),
+        out_specs=VMEM,
         compiler_params=PARAMS,
     )(order, *arrays)
 
@@ -94,27 +93,28 @@
         in_specs=[VMEM],
         out_specs=VMEM,
         compiler_params=PARAMS,
+        cost_estimate=pl.CostEstimate(flops=50_000_000_000, bytes_accessed=1 << 20, transcendentals=1 << 20),
     )(arrived)
 
 
 def spatial_kernel(frames, base_ref, kb_ref, bc_ref, q_ref, *refs):
-    (k0, v0, km1, vm1, kp1, vp1, km2, vm2, kp2, vp2, o_ref, m_ref, l_ref, acc_ref) = refs
+    (own, m1, p1, m2, p2, o_ref, m_ref, l_ref, acc_ref) = refs
     pieces = q_ref.shape[0] // 2
-    rows, depth = q_ref.shape[2:]
+    rows, depth = q_ref.shape[3:]
     size = pieces * rows
     factor = depth ** (-0.5) * math.log2(math.e)
     base = base_ref[0]
     slots = {
-        -3: (km2, vm2, 0),
-        -2: (km1, vm1, 0),
-        -1: (km1, vm1, pieces),
-        0: (k0, v0, 0),
-        1: (k0, v0, pieces),
-        2: (kp1, vp1, 0),
-        3: (kp1, vp1, pieces),
-        4: (kp2, vp2, 0),
+        -3: (m2, 0),
+        -2: (m1, 0),
+        -1: (m1, pieces),
+        0: (own, 0),
+        1: (own, pieces),
+        2: (p1, 0),
+        3: (p1, pieces),
+        4: (p2, 0),
     }
-    heads = q_ref.shape[1]
+    heads = q_ref.shape[2]
     for mine in range(2):
         frame = base + mine
         count = bc_ref[frame]
@@ -128,18 +128,18 @@
             return hit
 
         for head in range(heads):
-            q = q_ref[mine * pieces : (mine + 1) * pieces, head].reshape(size, depth)
+            q = q_ref[mine * pieces : (mine + 1) * pieces, 0, head].reshape(size, depth)
 
             def scores(slot):
-                k_ref, _, at = slots[slot]
-                k = k_ref[at : at + pieces, head].reshape(size, depth)
+                src, at = slots[slot]
+                k = src[at : at + pieces, 0, head].reshape(size, depth)
                 return lax.dot_general(
                     q, k, (((1,), (1,)), ((), ())), preferred_element_type=F32
                 )
 
             def value(slot):
-                _, v_ref, at = slots[slot]
-                return v_ref[at : at + pieces, head].reshape(size, depth)
+                src, at = slots[slot]
+                return src[at : at + pieces, 1, head].reshape(size, depth)
 
             s = scores(mine) * factor
             top = jnp.max(s, axis=1, keepdims=True)
@@ -170,10 +170,11 @@
 
 
 def spatial_attend(base, kb, bc, q, parts, frames):
-    size = q.shape[0] // 2 * q.shape[2]
+    dests, _, heads, rows, depth = q.shape
+    size = dests // 2 * rows
     return pl.pallas_call(
         functools.partial(spatial_kernel, frames),
-        out_shape=jax.ShapeDtypeStruct(q.shape, BF),
+        out_shape=jax.ShapeDtypeStruct((dests, heads, rows, depth), BF),
         in_specs=[SMEM] * 3 + [VMEM] * (1 + len(parts)),
         out_specs=VMEM,
         scratch_shapes=[
@@ -227,23 +228,19 @@
     base = (lax.axis_index("grp") * lax.axis_size("y") + lax.axis_index("y")) * 2
     base = base.astype(jnp.int32).reshape(1)
 
-    sk, sv = pack_spatial(head_order, (keys, values), dests, share)
-    k0 = exchange(sk, ("zl", "x"))
-    v0 = exchange(sv, ("zl", "x"))
-    (sq,) = pack_spatial(head_order, (queries,), dests, share)
     st = pack_temporal(head_order, queries, keys, values, items)
-    kp1, vp1 = from_block(k0, 1), from_block(v0, 1)
-    km1, vm1 = from_block(k0, -1), from_block(v0, -1)
-    kp2, vp2 = from_block(k0[:quarters], 2), from_block(v0[:quarters], 2)
-    km2, vm2 = from_block(k0[quarters:], -2), from_block(v0[quarters:], -2)
+    kv = exchange(pack_spatial(head_order, (keys, values), dests, share), ("zl", "x"))
+    kv, st = lax.optimization_barrier((kv, st))
     at = exchange(st, ("grp", "y", "zl"))
-    q0 = exchange(sq, ("zl", "x"))
+    p1 = from_block(kv, 1)
+    m1 = from_block(kv, -1)
+    p2 = from_block(kv[:quarters], 2)
+    m2 = from_block(kv[quarters:], -2)
+    at, sq = lax.optimization_barrier((at, pack_spatial(head_order, (queries,), dests, share)))
+    qs = exchange(sq, ("zl", "x"))
     to = temporal_attend(at)
     tr = exchange(to, ("grp", "y", "zl"))
-    so = spatial_attend(
-        base, key_blocks, block_count, q0,
-        (k0, v0, km1, vm1, kp1, vp1, km2, vm2, kp2, vp2), frames,
-    )
+    so = spatial_attend(base, key_blocks, block_count, qs, (kv, m1, p1, m2, p2), frames)
     sr = exchange(so, ("zl", "x"))
     return assemble(head_order, tr, sr, rows, width)
 

time: 185 us -> 148 us (0.80)
  the two profiles are of different devices: /device:TPU:48 before, /device:TPU:1 now
where the time goes in v2:
time: 148 us; the launch traced here: 145 us
  starting transfers between devices  56 us (38%)
  waiting for transfers between devices  40.9 us (28%)
  Pallas kernels  29.4 us (20%)
  blocking collectives  11.2 us (8%)
  local copies, waits for them, and re-layouts  7.31 us (5%)
    all_to_all x4, starting transfers between devices, exchange(): return lax.all_to_all(array, axes, 0, 0, tiled=True)  42.7 us
    all_to_all x4, waiting for transfers between devices, exchange(): return lax.all_to_all(array, axes, 0, 0, tiled=True)  40.9 us
    pallas_call x1, Pallas kernels, spatial_attend(): pl.pallas_call(functools.partial(spatial_kernel, frames), out_shape=jax.S...  19.6 us
    ppermute x4, starting transfers between devices, from_block(): lax.ppermute(array, ('grp', 'y'), [((i + by) % count, i) for i in range(c...  13.4 us
    all_to_all x1, blocking collectives, exchange(): return lax.all_to_all(array, axes, 0, 0, tiled=True)  11.2 us
    unnamed x25, local copies, waits for them, and re-layouts  6.25 us
    pallas_call x2, Pallas kernels, pack_spatial(): pl.pallas_call(pack_spatial_kernel, out_shape=jax.ShapeDtypeStruct((dests...  3.29 us
    pallas_call x1, Pallas kernels, temporal_attend(): pl.pallas_call(temporal_kernel, out_shape=jax.ShapeDtypeStruct((frames, i...  3.24 us
  transfers between devices with their start and end apart: 8, of which 3 were waited for; matrix products, arithmetic and copies ran while one was open for 1% of the time, Pallas kernels for 18%

profile of v2, /device:TPU:1, one launch (start us, length us, event | category | flops | bytes accessed | tf_op | source)
XLA Modules:
  0.0 145.0 jit_solution(2329924230400699862)
XLA Ops:
  0.0 0.0 copy-start.1
  0.0 1.1 copy-done.1
  1.1 0.0 copy-start.3
  1.1 1.1 copy-done.3
  2.3 0.0 copy-start.8
  2.3 0.7 copy-done.8
  2.9 0.0 copy-start.4
  2.9 1.8 %shard_map.64 = bf16[8,2,2,128,128]{4,3,2,1,0:T(8,128)(2,1)} custom-call(s32[24]{0:T(128)S(1)} %copy-done.8, bf16[128,3072]{1,0:T(8,128)(2,1)S(1)} %copy-done.1, bf16[128,3072]{1,0:T(8,128)(2,1)S(1)} %copy-done.3), custom_call_target="tpu_custom_call" | custom-call | tf_op jit(solution)/shard_map/pallas_call | solution.py:39
  4.7 0.0 copy-start
  4.7 0.0 copy-start.2
  4.7 6.8 %all-to-all-start = ((bf16[8,2,2,128,128]{4,3,2,1,0:T(8,128)(2,1)}), bf16[8,2,2,128,128]{4,3,2,1,0:T(8,128)(2,1)S(1)}, u32[]{:S(2)}, u32[]{:S(2)}) async-start(bf16[8,2,2,128,128]{4,3,2,1,0:T(8,128)(2,1)} %shard_map.64), calls=%async_computation | async-start | bytes 2097152 | tf_op jit(solution)/shard_map/all_to_all | solution.py:212
  11.5 0.0 copy-done.4
  11.5 0.0 copy-done
  11.5 0.0 copy-done.2
  11.6 0.0 copy-done.9
  11.6 1.6 %shard_map.65 = bf16[128,3,8,128]{3,2,1,0:T(8,128)(2,1)} custom-call(s32[24]{0:T(128)S(1)} %copy-done.9, bf16[128,3072]{1,0:T(8,128)(2,1)S(1)} %copy-done, bf16[128,3072]{1,0:T(8,128)(2,1)S(1)} %copy-done.2, bf16[128,3072]{1,0:T(8,128)(2,1)S(1)} %copy-done.4), custom_call_target="tpu_custom_call" | custom-call | tf_op jit(solution)/shard_map/pallas_call | solution.py:58
  13.2 8.4 %all-to-all-done.refs_0_ = bf16[8,2,2,128,128]{4,3,2,1,0:T(8,128)(2,1)S(1)} async-done(((bf16[8,2,2,128,128]{4,3,2,1,0:T(8,128)(2,1)}), bf16[8,2,2,128,128]{4,3,2,1,0:T(8,128)(2,1)S(1)}, u32[]{:S(2)}, u32[]{:S(2)}) %all-to-all-start) | async-done | bytes 1048608 | tf_op jit(solution)/shard_map/all_to_all | solution.py:212
  21.6 22.1 %all-to-all-start.1 = ((bf16[128,3,8,128]{3,2,1,0:T(8,128)(2,1)}), bf16[128,3,8,128]{3,2,1,0:T(8,128)(2,1)}, u32[]{:S(2)}, u32[]{:S(2)}) async-start(bf16[128,3,8,128]{3,2,1,0:T(8,128)(2,1)} %shard_map.65), calls=%async_computation.1 | async-start | bytes 1572864 | tf_op jit(solution)/shard_map/all_to_all | solution.py:212
  43.7 1.5 %shard_map.66 = bf16[8,1,2,128,128]{4,3,2,1,0:T(8,128)(2,1)} custom-call(s32[24]{0:T(128)S(1)} %copy-done.9, bf16[128,3072]{1,0:T(8,128)(2,1)S(1)} %copy-done), custom_call_target="tpu_custom_call" | custom-call | tf_op jit(solution)/shard_map/pallas_call | solution.py:39
  45.2 4.7 %collective-permute-start.1 = (bf16[8,2,2,128,128]{4,3,2,1,0:T(8,128)(2,1)S(1)}, bf16[8,2,2,128,128]{4,3,2,1,0:T(8,128)(2,1)S(1)}, u32[]{:S(2)}, u32[]{:S(2)}) collective-permute-start(bf16[8,2,2,128,128]{4,3,2,1,0:T(8,128)(2,1)S(1)} %all-to-all-done.refs_0_), channel_id=1, source_target_pairs={{8,0},{16,8},{24,16},{32,24},{40,32},{48,40},{56,48},{64,56},{72,6... | collective-permute-start | bytes 3145736 | tf_op jit(solution)/shard_map/ppermute | solution.py:217
  49.9 1.9 %collective-permute-start = (bf16[8,2,2,128,128]{4,3,2,1,0:T(8,128)(2,1)S(1)}, bf16[8,2,2,128,128]{4,3,2,1,0:T(8,128)(2,1)}, u32[]{:S(2)}, u32[]{:S(2)}) collective-permute-start(bf16[8,2,2,128,128]{4,3,2,1,0:T(8,128)(2,1)S(1)} %all-to-all-done.refs_0_), channel_id=1, source_target_pairs={{504,0},{0,8},{8,16},{16,24},{24,32},{32,40},{40,48},{48,56},{56,6... | collective-permute-start | bytes 3145736 | tf_op jit(solution)/shard_map/ppermute | solution.py:217
  51.9 1.1 fusion
  52.9 4.8 %collective-permute-start.3 = (bf16[4,2,2,128,128]{4,3,2,1,0:T(8,128)(2,1)}, bf16[4,2,2,128,128]{4,3,2,1,0:T(8,128)(2,1)S(1)}, u32[]{:S(2)}, u32[]{:S(2)}) collective-permute-start(bf16[4,2,2,128,128]{4,3,2,1,0:T(8,128)(2,1)} %get-tuple-element.13), channel_id=1, source_target_pairs={{16,0},{24,8},{32,16},{40,24},{48,32},{56,40},{64,48},{72,56},{80,... | collective-permute-start | bytes 1572872 | tf_op jit(solution)/shard_map/ppermute | solution.py:217
  57.7 1.9 %collective-permute-start.2 = (bf16[4,2,2,128,128]{4,3,2,1,0:T(8,128)(2,1)}, bf16[4,2,2,128,128]{4,3,2,1,0:T(8,128)(2,1)}, u32[]{:S(2)}, u32[]{:S(2)}) collective-permute-start(bf16[4,2,2,128,128]{4,3,2,1,0:T(8,128)(2,1)} %get-tuple-element.14), channel_id=1, source_target_pairs={{496,0},{504,8},{0,16},{8,24},{16,32},{24,40},{32,48},{40,56},{48,... | collective-permute-start | bytes 1572872 | tf_op jit(solution)/shard_map/ppermute | solution.py:217
  59.7 8.5 %all-to-all-done.1.in_ref = bf16[128,3,8,128]{3,2,1,0:T(8,128)(2,1)} async-done(((bf16[128,3,8,128]{3,2,1,0:T(8,128)(2,1)}), bf16[128,3,8,128]{3,2,1,0:T(8,128)(2,1)}, u32[]{:S(2)}, u32[]{:S(2)}) %all-to-all-start.1) | async-done | bytes 786464 | tf_op jit(solution)/shard_map/all_to_all | solution.py:212
  68.2 3.9 %all-to-all-start.3 = ((bf16[8,1,2,128,128]{4,3,2,1,0:T(8,128)(2,1)}), bf16[8,1,2,128,128]{4,3,2,1,0:T(8,128)(2,1)S(1)}, u32[]{:S(2)}, u32[]{:S(2)}) async-start(bf16[8,1,2,128,128]{4,3,2,1,0:T(8,128)(2,1)} %shard_map.66), calls=%async_computation.3 | async-start | bytes 1048576 | tf_op jit(solution)/shard_map/all_to_all | solution.py:212
  72.1 3.2 %shard_map.67 = bf16[128,8,128]{2,1,0:T(8,128)(2,1)S(1)} custom-call(bf16[128,3,8,128]{3,2,1,0:T(8,128)(2,1)} %all-to-all-done.1.in_ref), custom_call_target="tpu_custom_call" | custom-call | flops 49999998976 | bytes 1048576 | tf_op jit(solution)/shard_map/pallas_call | solution.py:90
  75.3 0.0 copy-start.7
  75.3 0.7 copy-done.7
  76.0 23.9 %all-to-all-done.3.q_ref = bf16[8,1,2,128,128]{4,3,2,1,0:T(8,128)(2,1)S(1)} async-done(((bf16[8,1,2,128,128]{4,3,2,1,0:T(8,128)(2,1)}), bf16[8,1,2,128,128]{4,3,2,1,0:T(8,128)(2,1)S(1)}, u32[]{:S(2)}, u32[]{:S(2)}) %all-to-all-start.3) | async-done | bytes 524320 | tf_op jit(solution)/shard_map/all_to_all | solution.py:212
  100.0 9.9 %all-to-all-start.2 = ((bf16[128,8,128]{2,1,0:T(8,128)(2,1)}), bf16[128,8,128]{2,1,0:T(8,128)(2,1)S(1)}, u32[]{:S(2)}, u32[]{:S(2)}) async-start(bf16[128,8,128]{2,1,0:T(8,128)(2,1)} %copy-done.7), calls=%async_computation.2 | async-start | bytes 524288 | tf_op jit(solution)/shard_map/all_to_all | solution.py:212
  109.9 0.0 copy-start.11
  109.9 0.7 copy-done.11
  110.6 0.1 copy.7.kb_ref
  110.7 0.0 copy-start.10
  110.7 0.0 collective-permute-done.3.refs_4_
  110.7 0.0 copy-start.5
  110.7 0.8 copy-done.5
  111.5 0.0 collective-permute-done.2.refs_3_
  111.5 0.0 collective-permute-done.1.refs_2_
  111.5 0.0 collective-permute-done.refs_1_
  111.5 0.0 copy-done.10
  111.5 0.0 copy-start.6
  111.5 1.0 copy-done.6
  112.6 19.6 %shard_map.68 = bf16[8,2,128,128]{3,2,1,0:T(8,128)(2,1)S(1)} custom-call(s32[1]{0:T(128)} %bitcast.base_ref, s32[128,6]{1,0:T(8,128)S(1)} %copy.7.kb_ref, s32[128]{0:T(128)S(1)} %copy-done.10, bf16[8,1,2,128,128]{4,3,2,1,0:T(8,128)(2,1)S(1)} %all-to-all-done.3.q_ref, bf16[8,2,2,128,128]{4,3,2,1,0:T(8,128)(2,1)S(1)} %all-to-all-done.refs_0_, ...), custom_call_target="tpu_custom_call" | custom-call | tf_op jit(solution)/shard_map/pallas_call | solution.py:175
  132.2 0.0 all-to-all-done.2.t_ref
  132.2 11.2 %all_to_all.25.s_ref = bf16[8,2,128,128]{3,2,1,0:T(8,128)(2,1)S(1)} all-to-all(bf16[8,2,128,128]{3,2,1,0:T(8,128)(2,1)S(1)} %shard_map.68), channel_id=1, replica_groups=mesh['grp'=8,'y'=8,'zl'=2,'x'=4] {'zl','x'}, dimensions={0} | all-to-all | bytes 1048576 | tf_op jit(solution)/shard_map/all_to_all | solution.py:212
  143.4 1.6 %shard_map.69 = bf16[128,3072]{1,0:T(8,128)(2,1)} custom-call(s32[24]{0:T(128)S(1)} %copy-done.9, bf16[128,8,128]{2,1,0:T(8,128)(2,1)S(1)} %all-to-all-done.2.t_ref, bf16[8,2,128,128]{3,2,1,0:T(8,128)(2,1)S(1)} %all_to_all.25.s_ref), custom_call_target="tpu_custom_call" | custom-call | tf_op jit(solution)/shard_map/pallas_call | solution.py:202
  (1 shorter events, 0.0 us)
Async XLA Ops:
  0.0 1.1 copy-start.1
  1.1 1.1 copy-start.3
  2.3 0.7 copy-start.8
  2.9 8.6 %copy-start.4 = (bf16[128,3072]{1,0:T(8,128)(2,1)S(1)}, bf16[128,3072]{1,0:T(8,128)(2,1)}, u32[]{:S(2)}) copy-start(bf16[128,3072]{1,0:T(8,128)(2,1)} %v_ref.1) | copy-start | bytes 2359300
  4.7 6.8 %copy-start = (bf16[128,3072]{1,0:T(8,128)(2,1)S(1)}, bf16[128,3072]{1,0:T(8,128)(2,1)}, u32[]{:S(2)}) copy-start(bf16[128,3072]{1,0:T(8,128)(2,1)} %refs_0_.3) | copy-start | bytes 2359300
  4.7 6.8 %copy-start.2 = (bf16[128,3072]{1,0:T(8,128)(2,1)S(1)}, bf16[128,3072]{1,0:T(8,128)(2,1)}, u32[]{:S(2)}) copy-start(bf16[128,3072]{1,0:T(8,128)(2,1)} %k_ref.1) | copy-start | bytes 2359300
  4.7 6.8 %copy-start.9 = (s32[24]{0:T(128)S(1)}, s32[24]{0:T(128)}, u32[]{:S(2)}) copy-start(s32[24]{0:T(128)} %order_ref.7) | copy-start | bytes 292
  4.7 16.9 %all-to-all-start = ((bf16[8,2,2,128,128]{4,3,2,1,0:T(8,128)(2,1)}), bf16[8,2,2,128,128]{4,3,2,1,0:T(8,128)(2,1)S(1)}, u32[]{:S(2)}, u32[]{:S(2)}) async-start(bf16[8,2,2,128,128]{4,3,2,1,0:T(8,128)(2,1)} %shard_map.64), calls=%async_computation | async-start | bytes 2097152 | tf_op jit(solution)/shard_map/all_to_all | solution.py:212
  21.6 46.6 %all-to-all-start.1 = ((bf16[128,3,8,128]{3,2,1,0:T(8,128)(2,1)}), bf16[128,3,8,128]{3,2,1,0:T(8,128)(2,1)}, u32[]{:S(2)}, u32[]{:S(2)}) async-start(bf16[128,3,8,128]{3,2,1,0:T(8,128)(2,1)} %shard_map.65), calls=%async_computation.1 | async-start | bytes 1572864 | tf_op jit(solution)/shard_map/all_to_all | solution.py:212
  45.2 66.3 %collective-permute-start.1 = (bf16[8,2,2,128,128]{4,3,2,1,0:T(8,128)(2,1)S(1)}, bf16[8,2,2,128,128]{4,3,2,1,0:T(8,128)(2,1)S(1)}, u32[]{:S(2)}, u32[]{:S(2)}) collective-permute-start(bf16[8,2,2,128,128]{4,3,2,1,0:T(8,128)(2,1)S(1)} %all-to-all-done.refs_0_), channel_id=1, source_target_pairs={{8,0},{16,8},{24,16},{32,24},{40,32},{48,40},{56,48},{64,56},{72,6... | collective-permute-start | bytes 3145736 | tf_op jit(solution)/shard_map/ppermute | solution.py:217
  49.9 61.6 %collective-permute-start = (bf16[8,2,2,128,128]{4,3,2,1,0:T(8,128)(2,1)S(1)}, bf16[8,2,2,128,128]{4,3,2,1,0:T(8,128)(2,1)}, u32[]{:S(2)}, u32[]{:S(2)}) collective-permute-start(bf16[8,2,2,128,128]{4,3,2,1,0:T(8,128)(2,1)S(1)} %all-to-all-done.refs_0_), channel_id=1, source_target_pairs={{504,0},{0,8},{8,16},{16,24},{24,32},{32,40},{40,48},{48,56},{56,6... | collective-permute-start | bytes 3145736 | tf_op jit(solution)/shard_map/ppermute | solution.py:217
  52.9 57.8 %collective-permute-start.3 = (bf16[4,2,2,128,128]{4,3,2,1,0:T(8,128)(2,1)}, bf16[4,2,2,128,128]{4,3,2,1,0:T(8,128)(2,1)S(1)}, u32[]{:S(2)}, u32[]{:S(2)}) collective-permute-start(bf16[4,2,2,128,128]{4,3,2,1,0:T(8,128)(2,1)} %get-tuple-element.13), channel_id=1, source_target_pairs={{16,0},{24,8},{32,16},{40,24},{48,32},{56,40},{64,48},{72,56},{80,... | collective-permute-start | bytes 1572872 | tf_op jit(solution)/shard_map/ppermute | solution.py:217
  57.7 53.8 %collective-permute-start.2 = (bf16[4,2,2,128,128]{4,3,2,1,0:T(8,128)(2,1)}, bf16[4,2,2,128,128]{4,3,2,1,0:T(8,128)(2,1)}, u32[]{:S(2)}, u32[]{:S(2)}) collective-permute-start(bf16[4,2,2,128,128]{4,3,2,1,0:T(8,128)(2,1)} %get-tuple-element.14), channel_id=1, source_target_pairs={{496,0},{504,8},{0,16},{8,24},{16,32},{24,40},{32,48},{40,56},{48,... | collective-permute-start | bytes 1572872 | tf_op jit(solution)/shard_map/ppermute | solution.py:217
  68.2 31.8 %all-to-all-start.3 = ((bf16[8,1,2,128,128]{4,3,2,1,0:T(8,128)(2,1)}), bf16[8,1,2,128,128]{4,3,2,1,0:T(8,128)(2,1)S(1)}, u32[]{:S(2)}, u32[]{:S(2)}) async-start(bf16[8,1,2,128,128]{4,3,2,1,0:T(8,128)(2,1)} %shard_map.66), calls=%async_computation.3 | async-start | bytes 1048576 | tf_op jit(solution)/shard_map/all_to_all | solution.py:212
  75.3 0.7 copy-start.7
  100.0 32.2 %all-to-all-start.2 = ((bf16[128,8,128]{2,1,0:T(8,128)(2,1)}), bf16[128,8,128]{2,1,0:T(8,128)(2,1)S(1)}, u32[]{:S(2)}, u32[]{:S(2)}) async-start(bf16[128,8,128]{2,1,0:T(8,128)(2,1)} %copy-done.7), calls=%async_computation.2 | async-start | bytes 524288 | tf_op jit(solution)/shard_map/all_to_all | solution.py:212
  109.9 0.7 copy-start.11
  110.7 0.8 copy-start.10
  110.7 0.8 copy-start.5
  111.5 1.0 copy-start.6
